TPU v7x, 512 devices: a whole 4x8x8 slice. The times are simulated.
512 devices in a mesh: seq: 128 (over y, x, z_lo), ch: 4 (over z_hi, core).
Axes of the slice: x: 4, y: 8, z: 8 (z_hi: 2, z_lo: 4; z = z_hi * 4 + z_lo), core: 2. Of those that a mesh axis runs over, the one named last changes fastest.
Arguments:
- bases: int32 [49152], P('seq'), may hold values from 0 to 3
- conv1_weight: bfloat16 [4, 15, 768], P(None, None, 'ch'), may hold values from -0.75 to 0.75
- gain1: float32 [768], P('ch'), may hold values from 0.5 to 1.5
- conv2_weight: bfloat16 [768, 5, 1024], P(None, None, 'ch'), may hold values from -0.09375 to 0.09375
- gain2: float32 [1024], P('ch'), may hold values from 0.5 to 1.5
- cotangent: bfloat16 [49152, 1024], P('seq', 'ch'), may hold values from -0.02734375 to 0.02734375
Outputs:
- features: bfloat16 [49152, 1024], P('seq', 'ch')
- grad_w1: float32 [4, 15, 768], P(None, None, 'ch')
- grad_gain1: float32 [768], P('ch')
- grad_w2: float32 [768, 5, 1024], P('seq', None, 'ch')
- grad_gain2: float32 [1024], P('ch')
All inputs are finite; a program needn't handle non-finite values.
Results may differ from a plain program's by a relative error of at most 0.019.
Values may be sent and summed in bfloat16 or wider, within the bound.
A program may use at most 64 MiB of HBM per device.

v0:
```python
import jax
import jax.numpy as jnp
from jax import lax
from jax.sharding import PartitionSpec as P

BASES = 4
KW1 = 15
KW2 = 5
D1 = 768
D2 = 1024


epsilon = 1e-06


def with_halo(block, sides, width):
    for axis, dim in sides:
        count = lax.axis_size(axis)
        forward = [(i, i + 1) for i in range(count - 1)]
        backward = [(target, source) for source, target in forward]
        low = lax.ppermute(
            lax.slice_in_dim(block, block.shape[dim] - width, None, axis=dim), axis, forward
        )
        high = lax.ppermute(lax.slice_in_dim(block, 0, width, axis=dim), axis, backward)
        block = jnp.concatenate([low, block, high], axis=dim)
    return block


def unfold_taps(padded, taps, count):
    pieces = [padded[:, tap : tap + count] for tap in range(taps)]
    stacked = jnp.stack(pieces, axis=1)
    return stacked.reshape(stacked.shape[0] * taps, count)


def contract_rows(left, right):
    return lax.dot_general(
        left, right, (((0,), (0,)), ((), ())), preferred_element_type=jnp.float32
    )


def contract_cols(left, right):
    return lax.dot_general(
        left, right, (((1,), (1,)), ((), ())), preferred_element_type=jnp.float32
    )


def on_device(bases, conv1_weight, gain1, conv2_weight, gain2, cotangent):
    positions = bases.shape[0]
    own1 = conv1_weight.shape[2]
    own2 = conv2_weight.shape[2]
    rim1 = KW1 // 2
    rim2 = KW2 // 2
    onehot_rows = (jnp.arange(BASES, dtype=jnp.int32)[:, None] == bases[None, :]).astype(
        jnp.bfloat16
    )
    flat_kernel = conv1_weight.reshape(BASES * KW1, own1)
    padded = with_halo(onehot_rows, (("seq", 1),), rim1)
    unfolded = unfold_taps(padded, KW1, positions)
    conv1_pre = contract_rows(unfolded, flat_kernel)
    square_sum = lax.psum(jnp.sum(conv1_pre * conv1_pre, axis=1), "ch")
    scale1 = lax.rsqrt(square_sum / D1 + epsilon)
    normed1 = conv1_pre * scale1[:, None]
    pre_act1 = normed1 * gain1
    act_own = jax.nn.gelu(pre_act1).astype(jnp.bfloat16)
    act_full = lax.all_gather(act_own, "ch", axis=1, tiled=True)
    act_rimmed = with_halo(act_full, (("seq", 0),), rim2)
    conv2_pre = jnp.zeros((positions, own2), jnp.float32)
    for tap in range(KW2):
        conv2_pre = conv2_pre + jnp.dot(
            act_rimmed[tap : tap + positions],
            conv2_weight[:, tap, :],
            preferred_element_type=jnp.float32,
        )
    square_two = lax.psum(jnp.sum(conv2_pre * conv2_pre, axis=1), "ch")
    scale2 = lax.rsqrt(square_two / D2 + epsilon)
    normed2 = conv2_pre * scale2[:, None]
    pre_act2 = normed2 * gain2
    features = jax.nn.gelu(pre_act2).astype(jnp.bfloat16)
    _, pull_two = jax.vjp(jax.nn.gelu, pre_act2)
    grad_pre2 = pull_two(cotangent.astype(jnp.float32))[0]
    gain2_part = jnp.sum(grad_pre2 * normed2, axis=0)
    grad_normed2 = grad_pre2 * gain2
    inner_two = lax.psum(jnp.sum(grad_normed2 * normed2, axis=1), "ch")
    grad_conv2 = (scale2[:, None] * (grad_normed2 - normed2 * (inner_two / D2)[:, None])).astype(
        jnp.bfloat16
    )

    def weight_rows():
        rows = [contract_rows(act_rimmed[tap : tap + positions], grad_conv2) for tap in range(KW2)]
        return jnp.stack(rows, axis=1)

    grad_w2 = lax.psum_scatter(weight_rows(), "seq", scatter_dimension=0, tiled=True)
    grad_rimmed = with_halo(grad_conv2, (("seq", 0),), rim2)
    partial_value = jnp.zeros((positions, D1), jnp.float32)
    for tap in range(KW2):
        offset = 2 * rim2 - tap
        partial_value = partial_value + contract_cols(
            grad_rimmed[offset : offset + positions], conv2_weight[:, tap, :]
        )
    grad_act = lax.psum_scatter(
        partial_value.astype(jnp.bfloat16), "ch", scatter_dimension=1, tiled=True
    ).astype(jnp.float32)
    _, pull_one = jax.vjp(jax.nn.gelu, pre_act1)
    grad_pre1 = pull_one(grad_act)[0]
    gain1_part = jnp.sum(grad_pre1 * normed1, axis=0)
    grad_normed1 = grad_pre1 * gain1
    inner_one = lax.psum(jnp.sum(grad_normed1 * normed1, axis=1), "ch")
    grad_conv1 = (scale1[:, None] * (grad_normed1 - normed1 * (inner_one / D1)[:, None])).astype(
        jnp.bfloat16
    )
    kernel_part = jnp.dot(unfolded, grad_conv1, preferred_element_type=jnp.float32).reshape(
        BASES, KW1, own1
    )
    grad_w1, grad_gain1, grad_gain2 = lax.psum((kernel_part, gain1_part, gain2_part), "seq")
    return (features, grad_w1, grad_gain1, grad_w2, grad_gain2)


def solution(mesh):
    in_specs = (
        P("seq"),
        P(None, None, "ch"),
        P("ch"),
        P(None, None, "ch"),
        P("ch"),
        P("seq", "ch"),
    )
    out_specs = (P("seq", "ch"), P(None, None, "ch"), P("ch"), P("seq", None, "ch"), P("ch"))
    return jax.shard_map(
        on_device, mesh=mesh, in_specs=in_specs, out_specs=out_specs, check_vma=False
    )
```

profile of v0, /device:TPU:32, one launch (start us, length us, event | category | flops | bytes accessed | tf_op | source)
XLA Modules:
  0.0 1555.1 jit_solution(18422960348985113731)
XLA Ops:
  8.1 0.7 fusion.69
  8.8 4.3 collective-permute-start
  13.1 7.6 collective-permute-start.1
  20.7 0.7 compare_convert_fusion
  21.4 0.1 fusion.95
  21.6 0.4 collective-permute-done.1
  22.0 0.1 fusion.94
  22.2 0.2 stack.78
  22.4 0.3 multiply_reduce_fusion.5
  22.6 17.0 %psum.49 = f32[384]{0:T(512)S(1)} all-reduce(f32[384]{0:T(512)S(1)} %get-tuple-element.114), channel_id=1, replica_groups=mesh['seq'=128,'ch'=4] {'ch'}, use_global_device_ids=true, to_apply=%region_1.0 | all-reduce | flops 384 | bytes 3072 | tf_op jit(solution)/shard_map/psum | solution.py:60
  39.7 0.9 multiply_convert_fusion.3
  40.6 10.8 all_gather.3
  51.4 0.1 fusion.105
  51.5 9.6 collective-permute-start.3
  61.1 1.4 fusion.32
  62.6 1.9 collective-permute-start.2
  64.5 1.3 collective-permute-done.3
  65.9 0.6 fusion.12
  66.5 10.9 collective-permute-done.2
  77.4 0.7 fusion.36
  78.1 0.6 fusion.9
  78.8 0.7 multiply_reduce_fusion.2
  79.5 10.8 psum.50
  90.4 0.5 multiply_reduce_fusion
  90.9 10.3 psum.51
  101.2 1.1 multiply_convert_fusion
  102.3 1.9 collective-permute-start.5
  104.2 1.4 fusion.30
  105.6 9.9 collective-permute-start.4
  115.6 0.4 fusion.25
  116.0 0.9 collective-permute-done.4
  116.9 0.4 fusion.34
  117.2 0.4 fusion.1
  117.7 1.3 fusion.2
  119.0 1.3 fusion.7
  120.3 1.3 fusion.6
  121.7 1.3 fusion.5
  123.0 1.3 fusion.4
  124.3 1.3 fusion.3
  125.6 1.3 dynamic-slice
  127.5 37.3 %reduce-scatter.3.cloned.1.call-done = bf16[384,192]{0,1:T(8,128)(2,1)} async-done(((bf16[384,768]{0,1:T(8,128)(2,1)}), bf16[384,192]{0,1:T(8,128)(2,1)}) %reduce-scatter.3.cloned.1.call-update) | async-done | bytes 147472 | tf_op jit(solution)/shard_map/reduce_scatter | solution.py:100
  164.9 1.3 multiply_reduce_fusion.3
  166.2 10.0 psum.52
  176.2 1.4 fusion.66
  177.6 723.5 %all-reduce.1 = (f32[4,15,192]{2,1,0:T(8,128)S(1)}, f32[192]{0:T(256)}, f32[256]{0:T(256)}) all-reduce(f32[4,15,192]{2,1,0:T(8,128)S(1)} %fusion.66, f32[192]{0:T(256)S(1)} %get-tuple-element.87, f32[256]{0:T(256)S(1)} %get-tuple-element.85), channel_id=1, replica_groups=mesh['seq'=128,'ch'=4] {'seq'}, use_global_device_ids=true, to_apply=%region_9.0 | all-reduce | flops 11968 | bytes 95744 | tf_op jit(solution)/shard_map/psum | solution.py:114
  901.1 0.7 copy.252
  901.8 644.4 %all-reduce.4.cloned.1.call-done = f32[768,5,256]{2,0,1:T(8,128)} async-done(((f32[768,5,256]{2,0,1:T(8,128)}), f32[768,5,256]{2,0,1:T(8,128)}) %all-reduce.4.cloned.1.call-update) | async-done | bytes 3932176
  1546.1 1.5 constant_dynamic-slice_fusion
  (40 shorter events, 0.5 us)
Async XLA Ops:
  8.0 14.4 copy-start
  8.0 156.8 %reduce-scatter.3.cloned.1.call-start = ((), (), s32[]{:S(2)}) async-start(), calls=%async_computation.1 | async-start | bytes 737280 | tf_op jit(solution)/shard_map/reduce_scatter | solution.py:100
  8.8 12.6 collective-permute-start
  13.1 8.9 collective-permute-start.1
  51.4 14.5 copy-start.1
  51.5 14.3 collective-permute-start.3
  62.6 14.9 collective-permute-start.2
  78.1 12.3 copy-start.3
  78.1 12.2 copy-start.4
  101.2 14.4 copy-start.2
  102.3 13.3 collective-permute-start.5
  105.6 11.2 collective-permute-start.4
  119.0 1427.1 %all-reduce.4.cloned.1.call-start = ((), (), s32[]{:S(2)}) async-start(), calls=%async_computation.2 | async-start | bytes 7864320
  125.6 39.3 %copy-start.5 = (f32[192]{0:T(256)S(1)}, f32[192]{0:T(256)}, u32[]{:S(2)}) copy-start(f32[192]{0:T(256)} %param.8) | copy-start | bytes 2308
Sparse Core Ops, SparseCore 0:
  119.1 45.6 reduce-scatter.2
Sparse Core Ops, SparseCore 1:
  125.7 1420.4 all-reduce.3
where the time goes:
time: 1560 us
  blocking collectives  782 us (50%)
  waiting for transfers between devices  695 us (45%)
  starting transfers between devices  35.4 us (2%)
  between operations  16.4 us (1%)
  matrix products  16.1 us (1%)
    psum x1, blocking collectives, on_device(): lax.psum((kernel_part, gain1_part, gain2_part), 'seq')  724 us
    unnamed x3, waiting for transfers between devices  644 us
    reduce_scatter x1, waiting for transfers between devices, on_device(): lax.psum_scatter(partial_value.astype(jnp.bfloat16), 'ch', scatter_dimens...  37.3 us
  transfers between devices with their start and end apart: 8, of which 6 were waited for; matrix products, arithmetic and copies ran while one was open for 1% of the time, Pallas kernels for 0%

commit v1 on v0

v1 whole, which is shorter than its diff:
```python
import math

import jax
import jax.numpy as jnp
from jax import lax
from jax.experimental import pallas as pl
from jax.experimental.pallas import tpu as pltpu
from jax.sharding import PartitionSpec as P

BASES = 4
KW1 = 15
KW2 = 5
D1 = 768
D2 = 1024
OWN1 = 192
OWN2 = 256
ROWS = 384
FRAME = 416
NX, NY, NZ, NC = 4, 8, 4, 4
NS = NX * NY * NZ
PART = ROWS // NC
CHUNK = 240
RA = 80
RB = CHUNK - RA
EPS = 1e-06
MESH = pl.DeviceIdType.MESH
F32 = jnp.float32
BF16 = jnp.bfloat16
ROOT = math.sqrt(2.0 / math.pi)

S_BASE, S_COT, S_W1, S_G1 = 0, 2, 4, 7
S_SQ, S_IN = 10, 13
S_CORE, S_ZHI, S_CH = 16, 18, 19
S_AY, S_BX, S_AX, S_BY, S_Z = 22, 29, 32, 35, 42
S_RX, S_RY, S_RZ = 45, 48, 55
N_SEM = 58


def gelu_parts(v):
    square = v * v
    t = jnp.tanh(ROOT * (v + 0.044715 * (square * v)))
    cdf = 0.5 * (1.0 + t)
    slope = cdf + (0.5 * ROOT) * v * (1.0 - t * t) * (1.0 + (3.0 * 0.044715) * square)
    return cdf, slope


def nt_dot(a, b):
    return lax.dot_general(a, b, (((1,), (1,)), ((), ())), preferred_element_type=F32)


def tn_dot(a, b):
    return lax.dot_general(a, b, (((0,), (0,)), ((), ())), preferred_element_type=F32)


def kernel(
    bases_ref, w1_ref, g1_ref, w2_ref, g2_ref, cot_ref,
    feat_ref, gw1_ref, gg1_ref, gw2_ref, gg2_ref,
    bext, cext, w1g, g1g, gain1, w1full, ut, uu, n1, s1, act, actt,
    w2v, ybuf, c2, dn2, q, s2, m2, sqs, ins, d2, dcat, g2acc, g1acc,
    pb, pcin, zs_, zr_, dc1, pay, chs, chr_, axs, ays, azs,
    big, rya, rxb, a2, b2, rxa, ryb, fin, zsl, rzl,
    ssem, rsem, lsem,
):
    s = lax.axis_index("seq")
    c = lax.axis_index("ch")
    z = lax.rem(s, NZ)
    x = lax.rem(lax.div(s, NZ), NX)
    y = lax.div(s, NZ * NX)
    core = lax.rem(c, 2)
    zh = lax.div(c, 2)

    def seq_of(yy, xx, zz):
        return (yy * NX + xx) * NZ + zz

    def x_peer(k):
        return lax.rem(x + k, NX)

    def y_peer(k):
        return lax.rem(y + k, NY)

    def z_peer(k):
        return lax.rem(z + k, NZ)

    def c_peer(k):
        return lax.rem(c + k, NC)

    right = lax.rem(s + 1, NS)
    left = lax.rem(s + NS - 1, NS)

    load_w2 = pltpu.make_async_copy(w2_ref, w2v, lsem.at[0])
    load_w2.start()
    load_cot = pltpu.make_async_copy(cot_ref, cext.at[pl.ds(16, ROWS)], lsem.at[1])
    load_cot.start()

    barrier = pltpu.get_barrier_semaphore()
    friends = [(right, c), (left, c)]
    friends += [(s, c_peer(k)) for k in range(1, NC)]
    friends += [(seq_of(y, x_peer(k), z), c) for k in range(1, NX)]
    friends += [(seq_of(y_peer(k), x, z), c) for k in range(1, NY)]
    friends += [(seq_of(y, x, z_peer(k)), c) for k in range(1, NZ)]
    for friend in friends:
        pl.semaphore_signal(barrier, inc=1, device_id=friend, device_id_type=MESH)
    pl.semaphore_wait(barrier, len(friends))

    pending = []

    def send(src, dst, number, to):
        copy = pltpu.make_async_remote_copy(
            src_ref=src,
            dst_ref=dst,
            send_sem=ssem.at[number],
            recv_sem=rsem.at[number],
            device_id=to,
            device_id_type=MESH,
        )
        copy.start()
        pending.append(copy)
        return copy

    def arrived(copies):
        for copy in copies:
            copy.wait_recv()

    got_bases = [
        send(bases_ref.at[:, pl.ds(256, 128)], bext.at[:, pl.ds(0, 128)], S_BASE, (right, c)),
        send(bases_ref.at[:, pl.ds(0, 128)], bext.at[:, pl.ds(512, 128)], S_BASE + 1, (left, c)),
    ]
    got_w1 = []
    for k in range(1, NC):
        to = (s, c_peer(k))
        got_w1.append(send(w1_ref, w1g.at[c], S_W1 + k - 1, to))
        got_w1.append(send(g1_ref, g1g.at[c], S_G1 + k - 1, to))
    got_cot = [
        send(cot_ref.at[pl.ds(ROWS - 16, 16)], cext.at[pl.ds(0, 16)], S_COT, (right, c)),
        send(cot_ref.at[pl.ds(0, 16)], cext.at[pl.ds(16 + ROWS, 16)], S_COT + 1, (left, c)),
    ]
    bext[:, pl.ds(128, ROWS)] = bases_ref[...]
    w1g[c] = w1_ref[...]
    g1g[c] = g1_ref[...]

    arrived(got_bases)
    place = lax.broadcasted_iota(jnp.int32, (1, 640), 1) - 128 + s * ROWS
    known = jnp.where((place >= 0) & (place < NS * ROWS), bext[...], -1)
    kinds = lax.broadcasted_iota(jnp.int32, (BASES, 512), 0)
    for tap in range(KW1):
        rolled = pltpu.roll(known, 640 - (105 + tap), 1)[:, :512]
        ut[pl.ds(BASES * tap, BASES), :] = (
            jnp.broadcast_to(rolled, (BASES, 512)) == kinds
        ).astype(F32)
    ut[pl.ds(BASES * KW1, 4), :] = jnp.zeros((4, 512), F32)
    for block in range(4):
        uu[pl.ds(128 * block, 128), :] = ut[:, pl.ds(128 * block, 128)].T.astype(BF16)

    arrived(got_w1)
    w1full[...] = jnp.concatenate(
        [w1g[k][:, :OWN1].astype(F32) for k in range(NC)], axis=1
    ).astype(BF16)
    gain1[...] = jnp.concatenate([g1g[k][:, :OWN1] for k in range(NC)], axis=1)
    n1[...] = jnp.dot(uu[pl.ds(0, FRAME), :], w1full[...], preferred_element_type=F32)

    @pl.loop(0, FRAME // 32)
    def _(i):
        rows = pl.ds(pl.multiple_of(i * 32, 32), 32)
        v = n1[rows, :]
        scale = lax.rsqrt(jnp.sum(v * v, axis=1, keepdims=True) * (1.0 / D1) + EPS)
        normed = v * scale
        n1[rows, :] = normed
        s1[rows, :] = jnp.broadcast_to(scale, (32, 128))
        pre = normed * gain1[...]
        cdf, _ = gelu_parts(pre)
        where = lax.broadcasted_iota(jnp.int32, (32, 1), 0) + (i * 32 - 16) + s * ROWS
        inside = (where >= 0) & (where < NS * ROWS)
        act[rows, :] = jnp.where(inside, pre * cdf, 0.0).astype(BF16)

    load_w2.wait()

    @pl.loop(0, KW2)
    def _(tap):
        ybuf[tap] = jnp.dot(act[...], w2v[tap], preferred_element_type=F32)

    pieces = [(8, 8)] + [(16 + 48 * k, 48) for k in range(8)] + [(400, 8)]
    q[pl.ds(0, 8), :] = jnp.zeros((8, 128), F32)
    q[pl.ds(408, 104), :] = jnp.zeros((104, 128), F32)
    for start, count in pieces:
        total = ybuf[0, pl.ds(start - 2, count), :]
        for tap in range(1, KW2):
            total = total + ybuf[tap, pl.ds(start + tap - 2, count), :]
        c2[pl.ds(start, count), :] = total
        lo, hi = total[:, :128], total[:, 128:]
        q[pl.ds(start, count), :] = lo * lo + hi * hi

    def row_sums(slots, number):
        for block in range(4):
            slots[c, :, pl.ds(128 * block, 128)] = jnp.sum(
                q[pl.ds(128 * block, 128), :].T, axis=0, keepdims=True
            )
        return [
            send(slots.at[c], slots.at[c], number + k - 1, (s, c_peer(k))) for k in range(1, NC)
        ]

    def spread(row, columns):
        for block in range(4):
            columns[pl.ds(128 * block, 128), :] = jnp.broadcast_to(
                row[:, 128 * block : 128 * block + 128], (128, 128)
            ).T

    got_sq = row_sums(sqs, S_SQ)
    for a in range(3):
        for b in range(6):
            tile = act[pl.ds(16 + 128 * a, 128), pl.ds(128 * b, 128)].astype(F32)
            actt[pl.ds(128 * b, 128), pl.ds(128 * a, 128)] = tile.T.astype(BF16)
    load_cot.wait()
    arrived(got_cot)
    arrived(got_sq)
    spread(
        lax.rsqrt((sqs[0] + sqs[1] + sqs[2] + sqs[3]) * (1.0 / D2) + EPS), s2
    )
    g2acc[...] = jnp.zeros_like(g2acc)

    def second_norm(rows, cot, own, count):
        scale = s2[rows, :]
        scale = jnp.concatenate([scale, scale], axis=1)
        normed = c2[rows, :] * scale
        gain = g2_ref[...]
        pre = normed * gain
        cdf, slope = gelu_parts(pre)
        dpre = cot * slope
        dnormed = dpre * gain
        inner = dnormed * normed
        c2[rows, :] = normed
        dn2[rows, :] = dnormed
        q[rows, :] = inner[:, :128] + inner[:, 128:]
        if own is not None:
            feat_ref[own, :] = (pre * cdf).astype(BF16)
            g2acc[...] += jnp.sum(dpre * normed, axis=0, keepdims=True)

    second_norm(pl.ds(8, 8), cext[pl.ds(0, 16), :].astype(F32)[8:16], None, 8)
    second_norm(pl.ds(400, 8), cext[pl.ds(400, 16), :].astype(F32)[0:8], None, 8)

    @pl.loop(0, 8)
    def _(i):
        rows = pl.ds(pl.multiple_of(16 + i * 48, 16), 48)
        own = pl.ds(pl.multiple_of(i * 48, 16), 48)
        second_norm(rows, cext[rows, :].astype(F32), own, 48)

    got_in = row_sums(ins, S_IN)
    arrived(got_in)
    spread((ins[0] + ins[1] + ins[2] + ins[3]) * (1.0 / D2), m2)

    for start, count in pieces:
        rows = pl.ds(start, count)
        scale, mean = s2[rows, :], m2[rows, :]
        scale = jnp.concatenate([scale, scale], axis=1)
        mean = jnp.concatenate([mean, mean], axis=1)
        grad = scale * (dn2[rows, :] - c2[rows, :] * mean)
        if start == 8:
            grad = jnp.where(s > 0, grad, 0.0)
        if start == 400:
            grad = jnp.where(s < NS - 1, grad, 0.0)
        d2[rows, :] = grad
    for tap in range(KW2):
        for k in range(8):
            dcat[pl.ds(48 * k, 48), pl.ds(256 * tap, 256)] = d2[
                pl.ds(48 * k + 18 - tap, 48), :
            ].astype(BF16)

    to_core = (s, zh * 2 + 1 - core)
    to_zhi = (s, (1 - zh) * 2 + core)
    got_core = []
    for j in range(4):
        part_of = lax.rem(zh + 1 - j // 2, 2) * 2 + lax.rem(core + 1 - j % 2, 2)
        rows = pl.ds(pl.multiple_of(part_of * PART, 32), PART)
        total = nt_dot(dcat[rows, pl.ds(0, 256)], w2v[0])
        for tap in range(1, KW2):
            total = total + nt_dot(dcat[rows, pl.ds(256 * tap, 256)], w2v[tap])
        pb[j] = total.astype(BF16)
        if j % 2 == 0:
            got_core.append(send(pb.at[j], pcin.at[j // 2], S_CORE + j // 2, to_core))
    arrived(got_core[:1])
    zs_[...] = (pb[1].astype(F32) + pcin[0].astype(F32)).astype(BF16)
    got_zhi = send(zs_, zr_, S_ZHI, to_zhi)

    def ay_copy(k):
        to = lax.rem(y + 1 + k, NY)
        return pltpu.make_async_remote_copy(
            src_ref=big.at[to, :, pl.ds(0, RA), :],
            dst_ref=rya.at[y],
            send_sem=ssem.at[S_AY + k],
            recv_sem=rsem.at[S_AY + k],
            device_id=(seq_of(to, x, z), c),
            device_id_type=MESH,
        )

    @pl.loop(0, NY)
    def _(k):
        to = lax.rem(y + 1 + k, NY)
        part = jnp.dot(
            actt[pl.ds(pl.multiple_of(to * 96, 32), 96), :],
            dcat[...],
            preferred_element_type=F32,
        )
        for xx in range(NX):
            for tap in range(KW2):
                lo = part[24 * xx : 24 * xx + 24, 256 * tap : 256 * tap + 128]
                hi = part[24 * xx : 24 * xx + 24, 256 * tap + 128 : 256 * tap + 256]
                big[to, xx, pl.ds(48 * tap, 48), :] = jnp.concatenate([lo, hi], axis=0).astype(BF16)

        @pl.when(k < NY - 1)
        def _():
            ay_copy(k).start()

    got_ay = [ay_copy(k) for k in range(NY - 1)]
    pending.extend(got_ay)
    got_bx = [
        send(
            big.at[:, x_peer(k), pl.ds(RA, RB), :],
            rxb.at[x],
            S_BX + k - 1,
            (seq_of(y, x_peer(k), z), c),
        )
        for k in range(1, NX)
    ]

    arrived(got_core[1:])
    arrived([got_zhi])
    g1acc[...] = jnp.zeros_like(g1acc)

    @pl.loop(0, PART // 32)
    def _(i):
        local = pl.ds(pl.multiple_of(i * 32, 32), 32)
        rows = pl.ds(pl.multiple_of(16 + c * PART + i * 32, 16), 32)
        dact = pb[3, local, :].astype(F32) + pcin[1, local, :].astype(F32) + zr_[local, :].astype(F32)
        normed = n1[rows, :]
        gain = gain1[...]
        _, slope = gelu_parts(normed * gain)
        dpre = dact * slope
        g1acc[...] += jnp.sum(dpre * normed, axis=0, keepdims=True)
        dnormed = dpre * gain
        mean = jnp.sum(dnormed * normed, axis=1, keepdims=True) * (1.0 / D1)
        dc1[local, :] = (s1[rows, :][:, :1] * (dnormed - normed * mean)).astype(BF16)

    mine = pl.ds(pl.multiple_of(16 + c * PART, 16), PART)
    pay[...] = tn_dot(uu[mine, :], dc1[...])
    pay[pl.ds(60, 1), :] = g1acc[...]
    for k in range(NC):
        chs[k, :, pl.ds(0, 128)] = pay[:, OWN1 * k : OWN1 * k + 128].astype(BF16)
        chs[k, :, pl.ds(128, 128)] = jnp.concatenate(
            [pay[:, OWN1 * k + 128 : OWN1 * k + 192], jnp.zeros((64, 64), F32)], axis=1
        ).astype(BF16)
    got_ch = [
        send(chs.at[c_peer(k)], chr_.at[c], S_CH + k - 1, (s, c_peer(k))) for k in range(1, NC)
    ]
    chr_[c] = chs[c]

    def add_up(slots, count):
        total = slots[0].astype(F32)
        for k in range(1, count):
            total = total + slots[k].astype(F32)
        return total

    rya[y] = big[y, :, pl.ds(0, RA), :]
    arrived(got_ay)

    @pl.loop(0, NX)
    def _(i):
        total = rya[0, i].astype(F32)
        for k in range(1, NY):
            total = total + rya[k, i].astype(F32)
        a2[i] = total.astype(BF16)

    got_ax = [
        send(a2.at[x_peer(k)], rxa.at[x], S_AX + k - 1, (seq_of(y, x_peer(k), z), c))
        for k in range(1, NX)
    ]
    rxa[x] = a2[x]
    rxb[x] = big[:, x, pl.ds(RA, RB), :]
    arrived(got_bx)

    @pl.loop(0, NY)
    def _(i):
        total = rxb[0, i].astype(F32)
        for k in range(1, NX):
            total = total + rxb[k, i].astype(F32)
        b2[i] = total.astype(BF16)

    got_by = [
        send(b2.at[y_peer(k)], ryb.at[y], S_BY + k - 1, (seq_of(y_peer(k), x, z), c))
        for k in range(1, NY)
    ]
    ryb[y] = b2[y]

    arrived(got_ch)
    small = add_up(chr_, NC)
    pay[:, pl.ds(0, 256)] = small
    pay[pl.ds(61, 1), pl.ds(0, 128)] = g2acc[:, :128]
    pay[pl.ds(62, 1), pl.ds(0, 128)] = g2acc[:, 128:]
    axs[x] = pay[:, pl.ds(0, 256)].astype(BF16)
    got_rx = [
        send(axs.at[x], axs.at[x], S_RX + k - 1, (seq_of(y, x_peer(k), z), c)) for k in range(1, NX)
    ]
    arrived(got_ax)
    fin[pl.ds(0, RA), :] = add_up(rxa, NX)
    arrived(got_rx)
    ays[y] = add_up(axs, NX).astype(BF16)
    got_ry = [
        send(ays.at[y], ays.at[y], S_RY + k - 1, (seq_of(y_peer(k), x, z), c)) for k in range(1, NY)
    ]
    arrived(got_by)
    fin[pl.ds(RA, RB), :] = add_up(ryb, NY)
    fin[pl.ds(CHUNK, 8), :] = jnp.zeros((8, 128), F32)
    for zz in range(NZ):
        for u in range(KW2):
            zsl[zz, pl.ds(16 * u, 16), :] = jnp.concatenate(
                [fin[pl.ds(48 * u + 6 * zz, 8), :], fin[pl.ds(48 * u + 24 + 6 * zz, 8), :]], axis=0
            ).astype(BF16)
    got_z = [
        send(zsl.at[z_peer(k)], rzl.at[z], S_Z + k - 1, (seq_of(y, x, z_peer(k)), c))
        for k in range(1, NZ)
    ]
    rzl[z] = zsl[z]
    arrived(got_ry)
    azs[z] = add_up(ays, NY).astype(BF16)
    got_rz = [
        send(azs.at[z], azs.at[z], S_RZ + k - 1, (seq_of(y, x, z_peer(k)), c)) for k in range(1, NZ)
    ]
    arrived(got_z)
    total = add_up(rzl, NZ)
    for tap in range(KW2):
        for half in range(2):
            gw2_ref[tap, :, pl.ds(128 * half, 128)] = total[16 * tap + 8 * half : 16 * tap + 8 * half + 6]
    arrived(got_rz)
    total = add_up(azs, NZ)
    gw1_ref[...] = total[:60, :OWN1]
    gg1_ref[...] = total[60:61, :OWN1]
    gg2_ref[:, pl.ds(0, 128)] = total[61:62, :128]
    gg2_ref[:, pl.ds(128, 128)] = total[62:63, :128]
    for copy in pending:
        copy.wait_send()


def on_device(bases, conv1_weight, gain1, conv2_weight, gain2, cotangent):
    w1 = conv1_weight.transpose(1, 0, 2).reshape(KW1 * BASES, OWN1)
    w1 = jnp.pad(w1, ((0, 4), (0, 64)))
    g1 = jnp.pad(gain1.reshape(1, OWN1), ((0, 0), (0, 64)))
    vmem = pl.BlockSpec(memory_space=pltpu.VMEM)
    hbm = pl.BlockSpec(memory_space=pl.ANY)
    V = pltpu.VMEM
    outs = pl.pallas_call(
        kernel,
        out_shape=(
            jax.ShapeDtypeStruct((ROWS, OWN2), BF16),
            jax.ShapeDtypeStruct((KW1 * BASES, OWN1), F32),
            jax.ShapeDtypeStruct((1, OWN1), F32),
            jax.ShapeDtypeStruct((KW2, 6, OWN2), F32),
            jax.ShapeDtypeStruct((1, OWN2), F32),
        ),
        in_specs=[vmem, vmem, vmem, hbm, vmem, hbm],
        out_specs=(vmem,) * 5,
        scratch_shapes=[
            V((1, 640), jnp.int32),
            V((FRAME, OWN2), BF16),
            V((NC, 64, 256), BF16),
            V((NC, 1, 256), F32),
            V((1, D1), F32),
            V((64, D1), BF16),
            V((64, 512), F32),
            V((512, 64), BF16),
            V((FRAME, D1), F32),
            V((FRAME, 128), F32),
            V((FRAME, D1), BF16),
            V((D1, ROWS), BF16),
            V((KW2, D1, OWN2), BF16),
            V((KW2, FRAME, OWN2), F32),
            V((FRAME, OWN2), F32),
            V((FRAME, OWN2), F32),
            V((512, 128), F32),
            V((512, 128), F32),
            V((512, 128), F32),
            V((NC, 1, 512), F32),
            V((NC, 1, 512), F32),
            V((FRAME, OWN2), F32),
            V((ROWS, KW2 * OWN2), BF16),
            V((1, OWN2), F32),
            V((1, D1), F32),
            V((4, PART, D1), BF16),
            V((2, PART, D1), BF16),
            V((PART, D1), BF16),
            V((PART, D1), BF16),
            V((PART, D1), BF16),
            V((64, D1), F32),
            V((NC, 64, 256), BF16),
            V((NC, 64, 256), BF16),
            V((NX, 64, 256), BF16),
            V((NY, 64, 256), BF16),
            V((NZ, 64, 256), BF16),
            V((NY, NX, CHUNK, 128), BF16),
            V((NY, NX, RA, 128), BF16),
            V((NX, NY, RB, 128), BF16),
            V((NX, RA, 128), BF16),
            V((NY, RB, 128), BF16),
            V((NX, RA, 128), BF16),
            V((NY, RB, 128), BF16),
            V((CHUNK + 8, 128), F32),
            V((NZ, 80, 128), BF16),
            V((NZ, 80, 128), BF16),
            pltpu.SemaphoreType.DMA((N_SEM,)),
            pltpu.SemaphoreType.DMA((N_SEM,)),
            pltpu.SemaphoreType.DMA((2,)),
        ],
        compiler_params=pltpu.CompilerParams(
            collective_id=0, has_side_effects=True, vmem_limit_bytes=44 * 1024 * 1024
        ),
        cost_estimate=pl.CostEstimate(
            flops=3 * 2 * ROWS * D1 * KW2 * OWN2, bytes_accessed=4 << 20, transcendentals=1 << 20
        ),
    )(
        bases.reshape(1, ROWS),
        w1,
        g1,
        conv2_weight.transpose(1, 0, 2),
        gain2.reshape(1, OWN2),
        cotangent,
    )
    features, gw1, gg1, gw2, gg2 = outs
    grad_w1 = gw1.reshape(KW1, BASES, OWN1).transpose(1, 0, 2)
    return (features, grad_w1, gg1.reshape(OWN1), gw2.transpose(1, 0, 2), gg2.reshape(OWN2))


def solution(mesh):
    in_specs = (
        P("seq"),
        P(None, None, "ch"),
        P("ch"),
        P(None, None, "ch"),
        P("ch"),
        P("seq", "ch"),
    )
    out_specs = (P("seq", "ch"), P(None, None, "ch"), P("ch"), P("seq", None, "ch"), P("ch"))
    return jax.shard_map(
        on_device, mesh=mesh, in_specs=in_specs, out_specs=out_specs, check_vma=False
    )
```

time: 1560 us -> 87.4 us (0.06)
  the two profiles are of different devices: /device:TPU:32 before, /device:TPU:16 now
where the time goes in v1:
time: 87.4 us; the launch traced here: 87.1 us
  Pallas kernels  78.1 us (89%)
  local copies, waits for them, and re-layouts  8.36 us (10%)
    pallas_call x1, Pallas kernels, on_device(): pl.pallas_call(kernel, out_shape=(jax.ShapeDtypeStruct((ROWS, OWN2), BF16...  78.1 us
    unnamed x10, local copies, waits for them, and re-layouts  5.56 us

profile of v1, /device:TPU:16, one launch (start us, length us, event | category | flops | bytes accessed | tf_op | source)
XLA Modules:
  0.0 87.1 jit_solution(12633746285645402745)
XLA Ops:
  0.6 0.7 pad.9.g1_ref
  1.3 0.7 reshape.31.bases_ref
  2.0 0.8 reshape.32
  2.8 0.0 copy-start
  2.8 1.5 %copy-done = bf16[768,5,256]{2,0,1:T(8,128)(2,1)S(1)} copy-done((bf16[768,5,256]{2,0,1:T(8,128)(2,1)S(1)}, bf16[768,5,256]{2,0,1:T(8,128)(2,1)}, u32[]{:S(2)}) %copy-start) | copy-done | bytes 1966104
  4.3 0.0 copy-start.1
  4.3 0.9 %copy-done.1 = bf16[384,256]{1,0:T(8,128)(2,1)S(1)} copy-done((bf16[384,256]{1,0:T(8,128)(2,1)S(1)}, bf16[384,256]{1,0:T(8,128)(2,1)}, u32[]{:S(2)}) %copy-start.1) | copy-done | bytes 196632
  5.3 0.0 copy-start.2
  5.3 0.7 copy-done.2
  6.0 78.1 %shard_map.101 = (bf16[384,256]{1,0:T(8,128)(2,1)S(1)}, f32[60,192]{1,0:T(8,128)S(1)}, f32[1,192]{1,0:T(1,128)S(1)}, f32[5,6,256]{2,1,0:T(8,128)S(1)}, f32[1,256]{1,0:T(1,128)S(1)}) custom-call(s32[1,384]{1,0:T(1,128)S(1)} %reshape.31.bases_ref, bf16[64,256]{1,0:T(8,128)(2,1)S(1)} %pad.8.w1_ref, f32[1,256]{1,0:T(1,128)S(1)} %pad.9.g1_ref, ...), custom_call_target="tpu_custom_call" | custom-call | flops 2264924160 | bytes 4194304 | tf_op jit(solution)/shard_map/pallas_call | solution.py:448
  84.1 0.6 reshape.35
  84.7 0.7 copy.15
  85.4 0.6 copy.16
  86.0 0.6 copy.17
  86.6 0.6 copy.18
  (1 shorter events, 0.0 us)
Async XLA Ops:
  2.8 1.5 %copy-start = (bf16[768,5,256]{2,0,1:T(8,128)(2,1)S(1)}, bf16[768,5,256]{2,0,1:T(8,128)(2,1)}, u32[]{:S(2)}) copy-start(bf16[768,5,256]{2,0,1:T(8,128)(2,1)} %param.9) | copy-start | bytes 5898244
  4.3 0.9 %copy-start.1 = (bf16[384,256]{1,0:T(8,128)(2,1)S(1)}, bf16[384,256]{1,0:T(8,128)(2,1)}, u32[]{:S(2)}) copy-start(bf16[384,256]{1,0:T(8,128)(2,1)} %cot_ref.1) | copy-start | bytes 589828
  5.3 0.7 copy-start.2

commit v2 on v1

v2 whole, which is shorter than its diff:
```python
import math

import jax
import jax.numpy as jnp
from jax import lax
from jax.experimental import pallas as pl
from jax.experimental.pallas import tpu as pltpu
from jax.sharding import PartitionSpec as P

BASES = 4
KW1 = 15
KW2 = 5
D1 = 768
D2 = 1024
OWN1 = 192
OWN2 = 256
ROWS = 384
FRAME = 416
NX, NY, NZ, NC = 4, 8, 4, 4
NS = NX * NY * NZ
TAPS1 = KW1 * BASES
WIDE = KW2 * OWN2
HALF = WIDE // 2
SHARE = D1 // NX
EPS = 1e-06
MESH = pl.DeviceIdType.MESH
F32 = jnp.float32
BF16 = jnp.bfloat16
ROOT = math.sqrt(2.0 / math.pi)

S_BASE, S_COT, S_W1, S_G1 = 0, 2, 4, 7
S_SQ, S_IN, S_CH = 10, 13, 16
S_ACT, S_D2, S_GY, S_Z = 19, 22, 28, 42
S_RX, S_RY, S_RZ, S_RG = 45, 48, 55, 58
N_SEM = 61


def gelu_parts(v):
    square = v * v
    t = jnp.tanh(ROOT * (v + 0.044715 * (square * v)))
    cdf = 0.5 * (1.0 + t)
    slope = cdf + (0.5 * ROOT) * v * (1.0 - t * t) * (1.0 + (3.0 * 0.044715) * square)
    return cdf, slope


def nt_dot(a, b):
    return lax.dot_general(a, b, (((1,), (1,)), ((), ())), preferred_element_type=F32)


def tn_dot(a, b):
    return lax.dot_general(a, b, (((0,), (0,)), ((), ())), preferred_element_type=F32)


def kernel(
    bases_hbm, w1_hbm, g1_hbm, w2_ref, g2_hbm, cot_ref,
    feat_ref, gw1_ref, gg1_ref, gw2_ref, gg2_ref,
    bases_ref, g1_ref, g2_ref, bext, cext, w1g, g1g, gain1, gain2, w1full, ut, uu, n1, s1, h1, act, actt, asel, aget,
    w2v, ybuf, c2, dn2, q, s2, m2, sqs, ins, d2, d2s, d2f, dcat, g2acc, g1acc,
    dact, dc1, pay, chs, chr_, rsend, rxs, rys, rzs, rgs,
    part, big, ryg, fin, zsl, rzl,
    ssem, rsem, lsem,
):
    s = lax.axis_index("seq")
    c = lax.axis_index("ch")
    z = lax.rem(s, NZ)
    x = lax.rem(lax.div(s, NZ), NX)
    y = lax.div(s, NZ * NX)

    def seq_of(yy, xx, zz):
        return (yy * NX + xx) * NZ + zz

    def x_peer(k):
        return lax.rem(x + k, NX)

    def y_peer(k):
        return lax.rem(y + k, NY)

    def z_peer(k):
        return lax.rem(z + k, NZ)

    def c_peer(k):
        return lax.rem(c + k, NC)

    right = lax.rem(s + 1, NS)
    left = lax.rem(s + NS - 1, NS)

    first_loads = [
        pltpu.make_async_copy(bases_hbm, bases_ref, lsem.at[11]),
        pltpu.make_async_copy(w1_hbm, w1g.at[c], lsem.at[12]),
        pltpu.make_async_copy(g1_hbm, g1_ref, lsem.at[13]),
        pltpu.make_async_copy(g2_hbm, g2_ref, lsem.at[14]),
    ]
    for load in first_loads:
        load.start()
    loads = []
    for half in range(2):
        for tap in range(KW2):
            n = half * KW2 + tap
            loads.append(
                pltpu.make_async_copy(
                    w2_ref.at[tap, :, pl.ds(128 * half, 128)],
                    w2v.at[:, pl.ds(128 * n, 128)],
                    lsem.at[n],
                )
            )
    for load in loads:
        load.start()
    load_cot = pltpu.make_async_copy(cot_ref, cext.at[pl.ds(16, ROWS)], lsem.at[10])
    load_cot.start()

    barrier = pltpu.get_barrier_semaphore()
    friends = [(right, c), (left, c)]
    friends += [(s, c_peer(k)) for k in range(1, NC)]
    friends += [(seq_of(y, x_peer(k), z), c) for k in range(1, NX)]
    friends += [(seq_of(y_peer(k), x, z), c) for k in range(1, NY)]
    friends += [(seq_of(y, x, z_peer(k)), c) for k in range(1, NZ)]
    for friend in friends:
        pl.semaphore_signal(barrier, inc=1, device_id=friend, device_id_type=MESH)
    for load in first_loads:
        load.wait()
    bext[:, pl.ds(128, ROWS)] = bases_ref[...].reshape(1, ROWS)
    g1g[c] = g1_ref[...].reshape(1, OWN1)
    gain2[...] = g2_ref[...].reshape(1, OWN2)
    pl.semaphore_wait(barrier, len(friends))

    pending = []

    def send(src, dst, number, to):
        copy = pltpu.make_async_remote_copy(
            src_ref=src,
            dst_ref=dst,
            send_sem=ssem.at[number],
            recv_sem=rsem.at[number],
            device_id=to,
            device_id_type=MESH,
        )
        copy.start()
        pending.append(copy)
        return copy

    def arrived(copies):
        for copy in copies:
            copy.wait_recv()

    got_bases = [
        send(bext.at[:, pl.ds(384, 128)], bext.at[:, pl.ds(0, 128)], S_BASE, (right, c)),
        send(bext.at[:, pl.ds(128, 128)], bext.at[:, pl.ds(512, 128)], S_BASE + 1, (left, c)),
    ]
    got_w1 = []
    for k in (2, 1, 3):
        to = (s, c_peer(k))
        got_w1.append(send(w1g.at[c], w1g.at[c], S_W1 + k - 1, to))
        got_w1.append(send(g1g.at[c], g1g.at[c], S_G1 + k - 1, to))
    got_cot = [
        send(cot_ref.at[pl.ds(ROWS - 16, 16)], cext.at[pl.ds(0, 16)], S_COT, (right, c)),
        send(cot_ref.at[pl.ds(0, 16)], cext.at[pl.ds(16 + ROWS, 16)], S_COT + 1, (left, c)),
    ]

    arrived(got_bases)
    place = lax.broadcasted_iota(jnp.int32, (1, 640), 1) - 128 + s * ROWS
    known = jnp.where((place >= 0) & (place < NS * ROWS), bext[...], -1)
    kinds = lax.broadcasted_iota(jnp.int32, (BASES, 512), 0)
    for tap in range(KW1):
        rolled = pltpu.roll(known, 640 - (105 + tap), 1)[:, :512]
        ut[pl.ds(BASES * tap, BASES), :] = (
            jnp.broadcast_to(rolled, (BASES, 512)) == kinds
        ).astype(F32)
    ut[pl.ds(BASES * KW1, 4), :] = jnp.zeros((4, 512), F32)
    for block in range(4):
        uu[pl.ds(128 * block, 128), :] = ut[:, pl.ds(128 * block, 128)].T.astype(BF16)

    arrived(got_w1)
    w1full[pl.ds(0, TAPS1), :] = jnp.concatenate(
        [w1g[k].astype(F32).reshape(TAPS1, OWN1) for k in range(NC)], axis=1
    ).astype(BF16)
    w1full[pl.ds(TAPS1, 4), :] = jnp.zeros((4, D1), BF16)
    gain1[...] = jnp.concatenate([g1g[k] for k in range(NC)], axis=1)
    n1[...] = jnp.dot(uu[pl.ds(0, FRAME), :], w1full[...], preferred_element_type=F32)

    @pl.loop(0, FRAME // 32)
    def _(i):
        rows = pl.ds(pl.multiple_of(i * 32, 32), 32)
        v = n1[rows, :]
        scale = lax.rsqrt(jnp.sum(v * v, axis=1, keepdims=True) * (1.0 / D1) + EPS)
        normed = v * scale
        n1[rows, :] = normed
        s1[rows, :] = jnp.broadcast_to(scale, (32, 128))
        pre = normed * gain1[...]
        cdf, _ = gelu_parts(pre)
        where = lax.broadcasted_iota(jnp.int32, (32, 1), 0) + (i * 32 - 16) + s * ROWS
        inside = (where >= 0) & (where < NS * ROWS)
        act[rows, :] = jnp.where(inside, pre * cdf, 0.0).astype(BF16)

    for load in loads:
        load.wait()
    ybuf[...] = jnp.dot(act[...], w2v[...], preferred_element_type=F32)
    pieces = [(8, 8)] + [(16 + 48 * k, 48) for k in range(8)] + [(400, 8)]
    q[pl.ds(0, 8), :] = jnp.zeros((8, 128), F32)
    q[pl.ds(408, 104), :] = jnp.zeros((104, 128), F32)
    for start, count in pieces:
        squares = None
        for half in range(2):
            total = None
            for tap in range(KW2):
                term = ybuf[
                    pl.ds(start + tap - 2, count), pl.ds(128 * (half * KW2 + tap), 128)
                ]
                total = term if total is None else total + term
            c2[pl.ds(start, count), pl.ds(128 * half, 128)] = total
            squares = total * total if squares is None else squares + total * total
        q[pl.ds(start, count), :] = squares
    def row_sums(slots, number):
        for block in range(4):
            slots[c, :, pl.ds(128 * block, 128)] = jnp.sum(
                q[pl.ds(128 * block, 128), :].T, axis=0, keepdims=True
            )
        return [
            send(slots.at[c], slots.at[c], number + k - 1, (s, c_peer(k))) for k in (2, 1, 3)
        ]

    def spread(row, columns):
        for block in range(4):
            columns[pl.ds(128 * block, 128), :] = jnp.broadcast_to(
                row[:, 128 * block : 128 * block + 128], (128, 128)
            ).T

    got_sq = row_sums(sqs, S_SQ)
    for a in range(3):
        for b in range(6):
            tile = act[pl.ds(16 + 128 * a, 128), pl.ds(128 * b, 128)].astype(F32)
            actt[pl.ds(128 * b, 128), pl.ds(128 * a, 128)] = tile.T
    for xx in range(NX):
        for yy in range(0, NY, 2):
            asel[xx, pl.ds(24 * yy, 48), :] = jnp.concatenate(
                [
                    actt[pl.ds(96 * yy + 24 * xx, 24), :],
                    actt[pl.ds(96 * yy + 96 + 24 * xx, 24), :],
                ],
                axis=0,
            ).astype(BF16)
    got_act = [
        send(asel.at[x_peer(k)], aget.at[x], S_ACT + k - 1, (seq_of(y, x_peer(k), z), c))
        for k in range(1, NX)
    ]
    aget[x] = asel[x]

    @pl.loop(0, ROWS // 32)
    def _(i):
        local = pl.ds(pl.multiple_of(i * 32, 32), 32)
        gain = gain1[...]
        _, slope = gelu_parts(n1[pl.ds(pl.multiple_of(i * 32 + 16, 16), 32), :] * gain)
        h1[local, :] = slope * gain

    load_cot.wait()
    arrived(got_cot)
    arrived(got_sq)
    spread(
        lax.rsqrt((sqs[0] + sqs[1] + sqs[2] + sqs[3]) * (1.0 / D2) + EPS), s2
    )
    g2acc[...] = jnp.zeros_like(g2acc)

    def second_norm(rows, cot, own, count):
        scale = s2[rows, :]
        scale = jnp.concatenate([scale, scale], axis=1)
        normed = c2[rows, :] * scale
        gain = gain2[...]
        pre = normed * gain
        cdf, slope = gelu_parts(pre)
        dpre = cot * slope
        dnormed = dpre * gain
        inner = dnormed * normed
        c2[rows, :] = normed
        dn2[rows, :] = dnormed
        q[rows, :] = inner[:, :128] + inner[:, 128:]
        if own is not None:
            feat_ref[own, :] = (pre * cdf).astype(BF16)
            g2acc[...] += jnp.sum(dpre * normed, axis=0, keepdims=True)

    second_norm(pl.ds(8, 8), cext[pl.ds(0, 16), :].astype(F32)[8:16], None, 8)
    second_norm(pl.ds(400, 8), cext[pl.ds(400, 16), :].astype(F32)[0:8], None, 8)

    @pl.loop(0, 8)
    def _(i):
        rows = pl.ds(pl.multiple_of(16 + i * 48, 16), 48)
        own = pl.ds(pl.multiple_of(i * 48, 16), 48)
        second_norm(rows, cext[rows, :].astype(F32), own, 48)

    got_in = row_sums(ins, S_IN)
    arrived(got_in)
    spread((ins[0] + ins[1] + ins[2] + ins[3]) * (1.0 / D2), m2)

    def rows_of(b):
        return pl.ds(pl.multiple_of(b * ROWS, 128), ROWS)

    def expand(b, half):
        for tap in range(KW2):
            for k in range(8):
                dcat[
                    pl.ds(pl.multiple_of(b * ROWS + 48 * k, 16), 48),
                    pl.ds(128 * (half * KW2 + tap), 128),
                ] = d2f[pl.ds(48 * k + 18 - tap, 48), :].astype(BF16)

    got_d2 = []
    for half in range(2):
        columns = pl.ds(128 * half, 128)
        d2[half, pl.ds(0, 8), :] = jnp.zeros((8, 128), F32)
        d2[half, pl.ds(408, 8), :] = jnp.zeros((8, 128), F32)
        for start, count in pieces:
            rows = pl.ds(start, count)
            grad = s2[rows, :] * (dn2[rows, columns] - c2[rows, columns] * m2[rows, :])
            if start == 8:
                grad = jnp.where(s > 0, grad, 0.0)
            if start == 400:
                grad = jnp.where(s < NS - 1, grad, 0.0)
            d2[half, rows, :] = grad
        d2s[x, half] = d2[half].astype(BF16)
        got_d2.append(
            [
                send(
                    d2s.at[x, half],
                    d2s.at[x, half],
                    S_D2 + 3 * half + k - 1,
                    (seq_of(y, x_peer(k), z), c),
                )
                for k in range(1, NX)
            ]
        )
    for half in range(2):
        d2f[...] = d2[half]
        expand(x, half)
    dact[...] = nt_dot(dcat[rows_of(x), :], w2v[...]).astype(BF16)
    g1acc[...] = jnp.zeros_like(g1acc)

    @pl.loop(0, ROWS // 32)
    def _(i):
        local = pl.ds(pl.multiple_of(i * 32, 32), 32)
        rows = pl.ds(pl.multiple_of(16 + i * 32, 16), 32)
        normed = n1[rows, :]
        dnormed = dact[local, :].astype(F32) * h1[local, :]
        inner = dnormed * normed
        g1acc[...] += jnp.sum(inner, axis=0, keepdims=True)
        mean = jnp.sum(inner, axis=1, keepdims=True) * (1.0 / D1)
        dc1[local, :] = (s1[rows, :][:, :1] * (dnormed - normed * mean)).astype(BF16)

    pay[...] = tn_dot(uu[pl.ds(16, ROWS), :], dc1[...])
    pay[pl.ds(60, 1), :] = g1acc[...] / gain1[...]
    for k in range(NC):
        chs[k, :, pl.ds(0, 128)] = pay[:, OWN1 * k : OWN1 * k + 128].astype(BF16)
        chs[k, :, pl.ds(128, 128)] = jnp.concatenate(
            [pay[:, OWN1 * k + 128 : OWN1 * k + 192], jnp.zeros((64, 64), F32)], axis=1
        ).astype(BF16)
    got_ch = [
        send(chs.at[c_peer(k)], chr_.at[c], S_CH + k - 1, (s, c_peer(k))) for k in (2, 1, 3)
    ]
    chr_[c] = chs[c]

    def add_up(slots, count):
        total = slots[0].astype(F32)
        for k in range(1, count):
            total = total + slots[k].astype(F32)
        return total

    def half_grad(half):
        arrived(got_d2[half])
        for k in range(1, NX):
            b = x_peer(k)
            d2f[...] = d2s[b, half].astype(F32)
            expand(b, half)
        columns = pl.ds(HALF * half, HALF)
        total = jnp.dot(aget[0], dcat[pl.ds(0, ROWS), columns], preferred_element_type=F32)
        for b in range(1, NX):
            total = total + jnp.dot(
                aget[b], dcat[pl.ds(ROWS * b, ROWS), columns], preferred_element_type=F32
            )
        part[...] = total
        for yy in range(NY):
            rows = pl.ds(24 * yy, 24)
            taps = [part[rows, pl.ds(128 * tap, 128)] for tap in range(KW2)]
            taps.append(jnp.zeros((8, 128), F32))
            for first in (0, 2, 4):
                piece = jnp.concatenate(taps[first : first + 2], axis=0).astype(BF16)
                big[half, yy, pl.ds(24 * first, piece.shape[0]), :] = piece
        copies = [
            send(
                big.at[half, y_peer(k)],
                ryg.at[half, y],
                S_GY + 7 * half + k - 1,
                (seq_of(y_peer(k), x, z), c),
            )
            for k in (4, 3, 5, 2, 6, 1, 7)
        ]
        ryg[half, y] = big[half, y]
        return copies

    arrived(got_act)
    got_y0 = half_grad(0)
    arrived(got_ch)
    pay[:, pl.ds(0, 256)] = add_up(chr_, NC)
    pay[pl.ds(61, 1), pl.ds(0, 128)] = g2acc[:, :128]
    pay[pl.ds(62, 1), pl.ds(0, 128)] = g2acc[:, 128:]
    for k in range(NX):
        rsend[k] = pay[pl.ds(16 * k, 16), pl.ds(0, 256)].astype(BF16)
    got_rx = [
        send(rsend.at[x_peer(k)], rxs.at[x], S_RX + k - 1, (seq_of(y, x_peer(k), z), c))
        for k in range(1, NX)
    ]
    rxs[x] = rsend[x]
    got_y1 = half_grad(1)
    arrived(got_rx)
    rys[y] = add_up(rxs, NX).astype(BF16)
    got_ry = [
        send(rys.at[y], rys.at[y], S_RY + k - 1, (seq_of(y_peer(k), x, z), c)) for k in range(1, NY)
    ]

    def half_sum(half):
        total = ryg[half, 0].astype(F32)
        for k in range(1, NY):
            total = total + ryg[half, k].astype(F32)
        fin[half] = total

    arrived(got_y0)
    half_sum(0)
    arrived(got_ry)
    rzs[z] = add_up(rys, NY).astype(BF16)
    got_rz = [
        send(rzs.at[z], rzs.at[z], S_RZ + k - 1, (seq_of(y, x, z_peer(k)), c)) for k in range(1, NZ)
    ]
    arrived(got_y1)
    half_sum(1)
    for zz in range(NZ):
        for tap in range(KW2):
            rows = pl.ds(24 * tap + 6 * zz, 8)
            zsl[zz, pl.ds(16 * tap, 16), :] = jnp.concatenate(
                [fin[0, rows, :], fin[1, rows, :]], axis=0
            ).astype(BF16)
    got_z = [
        send(zsl.at[z_peer(k)], rzl.at[z], S_Z + k - 1, (seq_of(y, x, z_peer(k)), c))
        for k in range(1, NZ)
    ]
    rzl[z] = zsl[z]
    arrived(got_rz)
    rgs[x] = add_up(rzs, NZ)
    got_rg = [
        send(rgs.at[x], rgs.at[x], S_RG + k - 1, (seq_of(y, x_peer(k), z), c)) for k in range(1, NX)
    ]
    arrived(got_z)
    total = add_up(rzl, NZ)
    for tap in range(KW2):
        for half in range(2):
            gw2_ref[tap, :, pl.ds(128 * half, 128)] = total[16 * tap + 8 * half : 16 * tap + 8 * half + 6]
    arrived(got_rg)
    for k in range(NX):
        for j in range(4):
            tap = 4 * k + j
            if tap < KW1:
                gw1_ref[tap] = rgs[k, pl.ds(4 * j, 4), pl.ds(0, OWN1)]
    gg1_ref[...] = rgs[3, pl.ds(12, 1), pl.ds(0, OWN1)].reshape(OWN1)
    gg2_ref[...] = jnp.concatenate(
        [rgs[3, pl.ds(13, 1), pl.ds(0, 128)], rgs[3, pl.ds(14, 1), pl.ds(0, 128)]], axis=1
    ).reshape(OWN2)
    for copy in pending:
        copy.wait_send()


def on_device(bases, conv1_weight, gain1, conv2_weight, gain2, cotangent):
    vmem = pl.BlockSpec(memory_space=pltpu.VMEM)
    hbm = pl.BlockSpec(memory_space=pl.ANY)
    V = pltpu.VMEM
    features, gw1, gg1, gw2, gg2 = pl.pallas_call(
        kernel,
        out_shape=(
            jax.ShapeDtypeStruct((ROWS, OWN2), BF16),
            jax.ShapeDtypeStruct((KW1, BASES, OWN1), F32),
            jax.ShapeDtypeStruct((OWN1,), F32),
            jax.ShapeDtypeStruct((KW2, 6, OWN2), F32),
            jax.ShapeDtypeStruct((OWN2,), F32),
        ),
        in_specs=[hbm] * 6,
        out_specs=(vmem,) * 5,
        scratch_shapes=[
            V((ROWS,), jnp.int32),
            V((OWN1,), F32),
            V((OWN2,), F32),
            V((1, 640), jnp.int32),
            V((FRAME, OWN2), BF16),
            V((NC, KW1, BASES, OWN1), BF16),
            V((NC, 1, OWN1), F32),
            V((1, D1), F32),
            V((1, OWN2), F32),
            V((64, D1), BF16),
            V((64, 512), F32),
            V((512, 64), BF16),
            V((FRAME, D1), F32),
            V((FRAME, 128), F32),
            V((ROWS, D1), F32),
            V((FRAME, D1), BF16),
            V((D1, ROWS), F32),
            V((NX, SHARE, ROWS), BF16),
            V((NX, SHARE, ROWS), BF16),
            V((D1, WIDE), BF16),
            V((FRAME, WIDE), F32),
            V((FRAME, OWN2), F32),
            V((FRAME, OWN2), F32),
            V((512, 128), F32),
            V((512, 128), F32),
            V((512, 128), F32),
            V((NC, 1, 512), F32),
            V((NC, 1, 512), F32),
            V((2, FRAME, 128), F32),
            V((NX, 2, FRAME, 128), BF16),
            V((FRAME, 128), F32),
            V((NX * ROWS, WIDE), BF16),
            V((1, OWN2), F32),
            V((1, D1), F32),
            V((ROWS, D1), BF16),
            V((ROWS, D1), BF16),
            V((64, D1), F32),
            V((NC, 64, 256), BF16),
            V((NC, 64, 256), BF16),
            V((NX, 16, 256), BF16),
            V((NX, 16, 256), BF16),
            V((NY, 16, 256), BF16),
            V((NZ, 16, 256), BF16),
            V((NX, 16, 256), F32),
            V((SHARE, HALF), F32),
            V((2, NY, 128, 128), BF16),
            V((2, NY, 128, 128), BF16),
            V((2, 128, 128), F32),
            V((NZ, 80, 128), BF16),
            V((NZ, 80, 128), BF16),
            pltpu.SemaphoreType.DMA((N_SEM,)),
            pltpu.SemaphoreType.DMA((N_SEM,)),
            pltpu.SemaphoreType.DMA((15,)),
        ],
        compiler_params=pltpu.CompilerParams(
            collective_id=0, has_side_effects=True, vmem_limit_bytes=58 * 1024 * 1024
        ),
        cost_estimate=pl.CostEstimate(
            flops=3 * 2 * ROWS * D1 * KW2 * OWN2, bytes_accessed=4 << 20, transcendentals=1 << 20
        ),
    )(
        bases,
        conv1_weight.transpose(1, 0, 2),
        gain1,
        conv2_weight.transpose(1, 0, 2),
        gain2,
        cotangent,
    )
    return (features, gw1.transpose(1, 0, 2), gg1, gw2.transpose(1, 0, 2), gg2)


def solution(mesh):
    in_specs = (
        P("seq"),
        P(None, None, "ch"),
        P("ch"),
        P(None, None, "ch"),
        P("ch"),
        P("seq", "ch"),
    )
    out_specs = (P("seq", "ch"), P(None, None, "ch"), P("ch"), P("seq", None, "ch"), P("ch"))
    return jax.shard_map(
        on_device, mesh=mesh, in_specs=in_specs, out_specs=out_specs, check_vma=False
    )
```

time: 87.4 us -> 74.5 us (0.85)
  the two profiles are of different devices: /device:TPU:16 before, /device:TPU:8 now
where the time goes in v2:
time: 74.5 us; the launch traced here: 74.2 us
  Pallas kernels  66.6 us (89%)
  local copies, waits for them, and re-layouts  6.95 us (9%)
    pallas_call x1, Pallas kernels, on_device(): pl.pallas_call(kernel, out_shape=(jax.ShapeDtypeStruct((ROWS, OWN2), BF16...  66.6 us
    unnamed x5, local copies, waits for them, and re-layouts  6.95 us

profile of v2, /device:TPU:8, one launch (start us, length us, event | category | flops | bytes accessed | tf_op | source)
XLA Modules:
  0.0 74.2 jit_solution(8227765506832283243)
XLA Ops:
  0.6 66.6 %shard_map.101 = (bf16[384,256]{1,0:T(8,128)(2,1)}, f32[15,4,192]{2,1,0:T(4,128)}, f32[192]{0:T(256)}, f32[5,6,256]{2,1,0:T(8,128)}, f32[256]{0:T(256)}) custom-call(s32[384]{0:T(512)} %bases_hbm.1, bf16[15,4,192]{2,1,0:T(4,128)(2,1)} %bitcast.7, f32[192]{0:T(256)} %g1_hbm.1, bf16[5,768,256]{2,1,0:T(8,128)(2,1)} %bitcast.6, f32[256]{0:T(256)} %g2_hbm.1, ...), custom_call_target="tpu_custom_call" | custom-call | flops 2264924160 | bytes 4194304 | tf_op jit(solution)/shard_map/pallas_call | solution.py:469
  67.3 1.6 %copy.16 = bf16[384,256]{1,0:T(8,128)(2,1)} copy(bf16[384,256]{1,0:T(8,128)(2,1)} %get-tuple-element.20) | data formatting | bytes 393216
  68.9 1.5 %copy.17 = f32[4,15,192]{2,0,1:T(4,128)} copy(f32[4,15,192]{2,0,1:T(4,128)} %bitcast.4) | data formatting | bytes 92160
  70.3 1.2 %copy.18 = f32[192]{0:T(256)} copy(f32[192]{0:T(256)} %get-tuple-element.22) | data formatting | bytes 1536
  71.6 1.4 %copy.19 = f32[6,5,256]{2,0,1:T(8,128)} copy(f32[6,5,256]{2,0,1:T(8,128)} %bitcast.5) | data formatting | bytes 61440
  73.0 1.2 %copy.20 = f32[256]{0:T(256)} copy(f32[256]{0:T(256)} %get-tuple-element.24) | data formatting | bytes 2048

commit v3 on v2

--- a/solution.py
+++ b/solution.py
@@ -380,6 +380,8 @@
             for first in (0, 2, 4):
                 piece = jnp.concatenate(taps[first : first + 2], axis=0).astype(BF16)
                 big[half, yy, pl.ds(24 * first, piece.shape[0]), :] = piece
+
+    def half_send(half):
         copies = [
             send(
                 big.at[half, y_peer(k)],
@@ -393,7 +395,8 @@
         return copies
 
     arrived(got_act)
-    got_y0 = half_grad(0)
+    half_grad(0)
+    got_y0 = half_send(0)
     arrived(got_ch)
     pay[:, pl.ds(0, 256)] = add_up(chr_, NC)
     pay[pl.ds(61, 1), pl.ds(0, 128)] = g2acc[:, :128]
@@ -405,12 +408,13 @@
         for k in range(1, NX)
     ]
     rxs[x] = rsend[x]
-    got_y1 = half_grad(1)
+    half_grad(1)
     arrived(got_rx)
     rys[y] = add_up(rxs, NX).astype(BF16)
     got_ry = [
         send(rys.at[y], rys.at[y], S_RY + k - 1, (seq_of(y_peer(k), x, z), c)) for k in range(1, NY)
     ]
+    got_y1 = half_send(1)
 
     def half_sum(half):
         total = ryg[half, 0].astype(F32)
@@ -418,12 +422,17 @@
             total = total + ryg[half, k].astype(F32)
         fin[half] = total
 
-    arrived(got_y0)
-    half_sum(0)
     arrived(got_ry)
     rzs[z] = add_up(rys, NY).astype(BF16)
     got_rz = [
         send(rzs.at[z], rzs.at[z], S_RZ + k - 1, (seq_of(y, x, z_peer(k)), c)) for k in range(1, NZ)
+    ]
+    arrived(got_y0)
+    half_sum(0)
+    arrived(got_rz)
+    rgs[x] = add_up(rzs, NZ)
+    got_rg = [
+        send(rgs.at[x], rgs.at[x], S_RG + k - 1, (seq_of(y, x_peer(k), z), c)) for k in range(1, NX)
     ]
     arrived(got_y1)
     half_sum(1)
@@ -438,11 +447,6 @@
         for k in range(1, NZ)
     ]
     rzl[z] = zsl[z]
-    arrived(got_rz)
-    rgs[x] = add_up(rzs, NZ)
-    got_rg = [
-        send(rgs.at[x], rgs.at[x], S_RG + k - 1, (seq_of(y, x_peer(k), z), c)) for k in range(1, NX)
-    ]
     arrived(got_z)
     total = add_up(rzl, NZ)
     for tap in range(KW2):
@@ -462,11 +466,19 @@
         copy.wait_send()
 
 
+def write_out(*refs):
+    copies = [pltpu.make_async_copy(refs[i], refs[5 + i], refs[10].at[i]) for i in range(5)]
+    for copy in copies:
+        copy.start()
+    for copy in copies:
+        copy.wait()
+
+
 def on_device(bases, conv1_weight, gain1, conv2_weight, gain2, cotangent):
     vmem = pl.BlockSpec(memory_space=pltpu.VMEM)
     hbm = pl.BlockSpec(memory_space=pl.ANY)
     V = pltpu.VMEM
-    features, gw1, gg1, gw2, gg2 = pl.pallas_call(
+    results = pl.pallas_call(
         kernel,
         out_shape=(
             jax.ShapeDtypeStruct((ROWS, OWN2), BF16),
@@ -546,6 +558,13 @@
         gain2,
         cotangent,
     )
+    features, gw1, gg1, gw2, gg2 = pl.pallas_call(
+        write_out,
+        out_shape=tuple(jax.ShapeDtypeStruct(r.shape, r.dtype) for r in results),
+        in_specs=[vmem] * 5,
+        out_specs=(hbm,) * 5,
+        scratch_shapes=[pltpu.SemaphoreType.DMA((5,))],
+    )(*results)
     return (features, gw1.transpose(1, 0, 2), gg1, gw2.transpose(1, 0, 2), gg2)
 
 

time: 74.5 us -> 67.2 us (0.902)
  the two profiles are of different devices: /device:TPU:8 before, /device:TPU:4 now
where the time goes in v3:
time: 67.2 us; the launch traced here: 67 us
  Pallas kernels  66.4 us (99%)
    pallas_call x1, Pallas kernels, on_device(): pl.pallas_call(kernel, out_shape=(jax.ShapeDtypeStruct((ROWS, OWN2), BF16...  64.7 us
    pallas_call x1, Pallas kernels, on_device(): pl.pallas_call(write_out, out_shape=tuple((jax.ShapeDtypeStruct(r.shape,...  1.75 us

profile of v3, /device:TPU:4, one launch (start us, length us, event | category | flops | bytes accessed | tf_op | source)
XLA Modules:
  0.0 67.0 jit_solution(14947111557625905640)
XLA Ops:
  0.6 64.7 %shard_map.101 = (bf16[384,256]{1,0:T(8,128)(2,1)}, f32[15,4,192]{2,1,0:T(4,128)}, f32[192]{0:T(256)}, f32[5,6,256]{2,1,0:T(8,128)}, f32[256]{0:T(256)}) custom-call(s32[384]{0:T(512)} %bases_hbm.1, bf16[15,4,192]{2,1,0:T(4,128)(2,1)} %bitcast.7, f32[192]{0:T(256)} %g1_hbm.1, bf16[5,768,256]{2,1,0:T(8,128)(2,1)} %bitcast.4, f32[256]{0:T(256)} %g2_hbm.1, ...), custom_call_target="tpu_custom_call" | custom-call | flops 2264924160 | bytes 4194304 | tf_op jit(solution)/shard_map/pallas_call | solution.py:481
  65.3 1.7 %shard_map.102 = (bf16[384,256]{1,0:T(8,128)(2,1)}, f32[15,4,192]{2,1,0:T(4,128)}, f32[192]{0:T(256)}, f32[5,6,256]{2,1,0:T(8,128)}, f32[256]{0:T(256)}) custom-call(bf16[384,256]{1,0:T(8,128)(2,1)} %get-tuple-element.15.refs_0_, f32[15,4,192]{2,1,0:T(4,128)} %get-tuple-element.16.refs_1_, f32[192]{0:T(256)} %get-tuple-element.17.refs_2_, ...), custom_call_target="tpu_custom_call" | custom-call | tf_op jit(solution)/shard_map/pallas_call | solution.py:561

commit v4 on v3

--- a/solution.py
+++ b/solution.py
@@ -30,9 +30,10 @@
 
 S_BASE, S_COT, S_W1, S_G1 = 0, 2, 4, 7
 S_SQ, S_IN, S_CH = 10, 13, 16
-S_ACT, S_D2, S_GY, S_Z = 19, 22, 28, 42
-S_RX, S_RY, S_RZ, S_RG = 45, 48, 55, 58
-N_SEM = 61
+S_ACT, S_D2 = 19, 22
+S_RX, S_RY, S_RZ, S_RG = 28, 31, 38, 41
+S_Y1, S_Z1, S_Z2, S_Y2 = 44, 58, 64, 70
+N_SEM = 84
 
 
 def gelu_parts(v):
@@ -57,7 +58,7 @@
     bases_ref, g1_ref, g2_ref, bext, cext, w1g, g1g, gain1, gain2, w1full, ut, uu, n1, s1, h1, act, actt, asel, aget,
     w2v, ybuf, c2, dn2, q, s2, m2, sqs, ins, d2, d2s, d2f, dcat, g2acc, g1acc,
     dact, dc1, pay, chs, chr_, rsend, rxs, rys, rzs, rgs,
-    part, big, ryg, fin, zsl, rzl,
+    part, zpack, zbig, rz0, yb, ry0, big, ryg, fin, zfin, zsl, rzl,
     ssem, rsem, lsem,
 ):
     s = lax.axis_index("seq")
@@ -373,30 +374,86 @@
                 aget[b], dcat[pl.ds(ROWS * b, ROWS), columns], preferred_element_type=F32
             )
         part[...] = total
+
+    def pack(half):
         for yy in range(NY):
             rows = pl.ds(24 * yy, 24)
-            taps = [part[rows, pl.ds(128 * tap, 128)] for tap in range(KW2)]
-            taps.append(jnp.zeros((8, 128), F32))
-            for first in (0, 2, 4):
-                piece = jnp.concatenate(taps[first : first + 2], axis=0).astype(BF16)
-                big[half, yy, pl.ds(24 * first, piece.shape[0]), :] = piece
-
-    def half_send(half):
+            taps = [part[rows, pl.ds(128 * tap, 128)] for tap in range(3)]
+            big[half, yy, pl.ds(0, 48), :] = jnp.concatenate(taps[:2], axis=0).astype(BF16)
+            big[half, yy, pl.ds(48, 32), :] = jnp.concatenate(
+                [taps[2], jnp.zeros((8, 128), F32)], axis=0
+            ).astype(BF16)
+            for zz in range(NZ):
+                for tap in (3, 4):
+                    zpack[zz, yy, pl.ds(6 * tap - 18, 6), :] = part[
+                        pl.ds(24 * yy + 6 * zz, 6), pl.ds(128 * tap, 128)
+                    ]
+        zpack[:, :, pl.ds(12, 4), :] = jnp.zeros((NZ, NY, 4, 128), F32)
+        zbig[half] = zpack[...].astype(BF16)
+
+    def y_sends(blocks, slots, half, number):
         copies = [
             send(
-                big.at[half, y_peer(k)],
-                ryg.at[half, y],
-                S_GY + 7 * half + k - 1,
+                blocks.at[half, y_peer(k)],
+                slots.at[half, y],
+                number + 7 * half + k - 1,
                 (seq_of(y_peer(k), x, z), c),
             )
             for k in (4, 3, 5, 2, 6, 1, 7)
         ]
-        ryg[half, y] = big[half, y]
+        slots[half, y] = blocks[half, y]
         return copies
+
+    def z_sends(blocks, slots, half, number):
+        copies = [
+            send(
+                blocks.at[half, z_peer(k)],
+                slots.at[half, z],
+                number + 3 * half + k - 1,
+                (seq_of(y, x, z_peer(k)), c),
+            )
+            for k in (2, 1, 3)
+        ]
+        slots[half, z] = blocks[half, z]
+        return copies
+
+    def add_half(slots, half, count):
+        total = slots[half, 0].astype(F32)
+        for k in range(1, count):
+            total = total + slots[half, k].astype(F32)
+        return total
+
+    def first_stage(half):
+        return y_sends(big, ryg, half, S_Y1), z_sends(zbig, rz0, half, S_Z1)
+
+    def second_stage(half, got):
+        arrived(got[1])
+        yb[half] = add_half(rz0, half, NZ).astype(BF16)
+        over_y = y_sends(yb, ry0, half, S_Y2)
+        arrived(got[0])
+        fin[...] = add_half(ryg, half, NY)
+        for zz in range(NZ):
+            for tap in range(3):
+                zfin[zz, pl.ds(6 * tap, 6), :] = fin[pl.ds(24 * tap + 6 * zz, 6), :]
+            zfin[zz, pl.ds(18, 14), :] = jnp.zeros((14, 128), F32)
+        zsl[half] = zfin[...].astype(BF16)
+        return over_y, z_sends(zsl, rzl, half, S_Z2)
+
+    def last_stage(half, got):
+        columns = pl.ds(128 * half, 128)
+        arrived(got[0])
+        total = add_half(ry0, half, NY)
+        for tap in (3, 4):
+            gw2_ref[tap, :, columns] = total[6 * tap - 18 : 6 * tap - 12]
+        arrived(got[1])
+        total = add_half(rzl, half, NZ)
+        for tap in range(3):
+            gw2_ref[tap, :, columns] = total[6 * tap : 6 * tap + 6]
 
     arrived(got_act)
     half_grad(0)
-    got_y0 = half_send(0)
+    pack(0)
+    first0 = first_stage(0)
     arrived(got_ch)
     pay[:, pl.ds(0, 256)] = add_up(chr_, NC)
     pay[pl.ds(61, 1), pl.ds(0, 128)] = g2acc[:, :128]
@@ -408,50 +465,29 @@
         for k in range(1, NX)
     ]
     rxs[x] = rsend[x]
-    half_grad(1)
     arrived(got_rx)
     rys[y] = add_up(rxs, NX).astype(BF16)
     got_ry = [
-        send(rys.at[y], rys.at[y], S_RY + k - 1, (seq_of(y_peer(k), x, z), c)) for k in range(1, NY)
-    ]
-    got_y1 = half_send(1)
-
-    def half_sum(half):
-        total = ryg[half, 0].astype(F32)
-        for k in range(1, NY):
-            total = total + ryg[half, k].astype(F32)
-        fin[half] = total
-
+        send(rys.at[y], rys.at[y], S_RY + k - 1, (seq_of(y_peer(k), x, z), c))
+        for k in (4, 3, 5, 2, 6, 1, 7)
+    ]
+    half_grad(1)
+    pack(1)
+    first1 = first_stage(1)
+    second0 = second_stage(0, first0)
     arrived(got_ry)
     rzs[z] = add_up(rys, NY).astype(BF16)
     got_rz = [
         send(rzs.at[z], rzs.at[z], S_RZ + k - 1, (seq_of(y, x, z_peer(k)), c)) for k in range(1, NZ)
     ]
-    arrived(got_y0)
-    half_sum(0)
+    second1 = second_stage(1, first1)
     arrived(got_rz)
     rgs[x] = add_up(rzs, NZ)
     got_rg = [
         send(rgs.at[x], rgs.at[x], S_RG + k - 1, (seq_of(y, x_peer(k), z), c)) for k in range(1, NX)
     ]
-    arrived(got_y1)
-    half_sum(1)
-    for zz in range(NZ):
-        for tap in range(KW2):
-            rows = pl.ds(24 * tap + 6 * zz, 8)
-            zsl[zz, pl.ds(16 * tap, 16), :] = jnp.concatenate(
-                [fin[0, rows, :], fin[1, rows, :]], axis=0
-            ).astype(BF16)
-    got_z = [
-        send(zsl.at[z_peer(k)], rzl.at[z], S_Z + k - 1, (seq_of(y, x, z_peer(k)), c))
-        for k in range(1, NZ)
-    ]
-    rzl[z] = zsl[z]
-    arrived(got_z)
-    total = add_up(rzl, NZ)
-    for tap in range(KW2):
-        for half in range(2):
-            gw2_ref[tap, :, pl.ds(128 * half, 128)] = total[16 * tap + 8 * half : 16 * tap + 8 * half + 6]
+    last_stage(0, second0)
+    last_stage(1, second1)
     arrived(got_rg)
     for k in range(NX):
         for j in range(4):
@@ -535,11 +571,17 @@
             V((NZ, 16, 256), BF16),
             V((NX, 16, 256), F32),
             V((SHARE, HALF), F32),
-            V((2, NY, 128, 128), BF16),
-            V((2, NY, 128, 128), BF16),
-            V((2, 128, 128), F32),
-            V((NZ, 80, 128), BF16),
-            V((NZ, 80, 128), BF16),
+            V((NZ, NY, 16, 128), F32),
+            V((2, NZ, NY, 16, 128), BF16),
+            V((2, NZ, NY, 16, 128), BF16),
+            V((2, NY, 16, 128), BF16),
+            V((2, NY, 16, 128), BF16),
+            V((2, NY, 80, 128), BF16),
+            V((2, NY, 80, 128), BF16),
+            V((80, 128), F32),
+            V((NZ, 32, 128), F32),
+            V((2, NZ, 32, 128), BF16),
+            V((2, NZ, 32, 128), BF16),
             pltpu.SemaphoreType.DMA((N_SEM,)),
             pltpu.SemaphoreType.DMA((N_SEM,)),
             pltpu.SemaphoreType.DMA((15,)),

time: 67.2 us -> 63.7 us (0.948)
  the two profiles are of different devices: /device:TPU:4 before, /device:TPU:8 now
where the time goes in v4:
time: 63.7 us; the launch traced here: 63.6 us
  Pallas kernels  62.9 us (99%)
  between operations  0.64 us (1%)
    pallas_call x1, Pallas kernels, on_device(): pl.pallas_call(kernel, out_shape=(jax.ShapeDtypeStruct((ROWS, OWN2), BF16...  61.2 us
    pallas_call x1, Pallas kernels, on_device(): pl.pallas_call(write_out, out_shape=tuple((jax.ShapeDtypeStruct(r.shape,...  1.75 us

profile of v4, /device:TPU:8, one launch (start us, length us, event | category | flops | bytes accessed | tf_op | source)
XLA Modules:
  0.0 63.6 jit_solution(9123608211431694393)
XLA Ops:
  0.6 61.2 %shard_map.101 = (bf16[384,256]{1,0:T(8,128)(2,1)}, f32[15,4,192]{2,1,0:T(4,128)}, f32[192]{0:T(256)}, f32[5,6,256]{2,1,0:T(8,128)}, f32[256]{0:T(256)}) custom-call(s32[384]{0:T(512)} %bases_hbm.1, bf16[15,4,192]{2,1,0:T(4,128)(2,1)} %bitcast.7, f32[192]{0:T(256)} %g1_hbm.1, bf16[5,768,256]{2,1,0:T(8,128)(2,1)} %bitcast.4, f32[256]{0:T(256)} %g2_hbm.1, ...), custom_call_target="tpu_custom_call" | custom-call | flops 2264924160 | bytes 4194304 | tf_op jit(solution)/shard_map/pallas_call | solution.py:517
  61.8 1.7 %shard_map.102 = (bf16[384,256]{1,0:T(8,128)(2,1)}, f32[15,4,192]{2,1,0:T(4,128)}, f32[192]{0:T(256)}, f32[5,6,256]{2,1,0:T(8,128)}, f32[256]{0:T(256)}) custom-call(bf16[384,256]{1,0:T(8,128)(2,1)} %get-tuple-element.15.refs_0_, f32[15,4,192]{2,1,0:T(4,128)} %get-tuple-element.16.refs_1_, f32[192]{0:T(256)} %get-tuple-element.17.refs_2_, ...), custom_call_target="tpu_custom_call" | custom-call | tf_op jit(solution)/shard_map/pallas_call | solution.py:603

commit v5 on v4

--- a/solution.py
+++ b/solution.py
@@ -346,10 +346,9 @@
     pay[...] = tn_dot(uu[pl.ds(16, ROWS), :], dc1[...])
     pay[pl.ds(60, 1), :] = g1acc[...] / gain1[...]
     for k in range(NC):
-        chs[k, :, pl.ds(0, 128)] = pay[:, OWN1 * k : OWN1 * k + 128].astype(BF16)
-        chs[k, :, pl.ds(128, 128)] = jnp.concatenate(
-            [pay[:, OWN1 * k + 128 : OWN1 * k + 192], jnp.zeros((64, 64), F32)], axis=1
-        ).astype(BF16)
+        chs[k, pl.ds(0, 64), :] = pay[:, OWN1 * k : OWN1 * k + 128].astype(BF16)
+        rest = pay[:, OWN1 * k + 128 : OWN1 * k + 192]
+        chs[k, pl.ds(64, 32), :] = jnp.concatenate([rest[:32], rest[32:]], axis=1).astype(BF16)
     got_ch = [
         send(chs.at[c_peer(k)], chr_.at[c], S_CH + k - 1, (s, c_peer(k))) for k in (2, 1, 3)
     ]
@@ -426,10 +425,11 @@
     def first_stage(half):
         return y_sends(big, ryg, half, S_Y1), z_sends(zbig, rz0, half, S_Z1)
 
-    def second_stage(half, got):
+    def second_stage(half, got, between):
         arrived(got[1])
         yb[half] = add_half(rz0, half, NZ).astype(BF16)
         over_y = y_sends(yb, ry0, half, S_Y2)
+        middle = between()
         arrived(got[0])
         fin[...] = add_half(ryg, half, NY)
         for zz in range(NZ):
@@ -437,7 +437,7 @@
                 zfin[zz, pl.ds(6 * tap, 6), :] = fin[pl.ds(24 * tap + 6 * zz, 6), :]
             zfin[zz, pl.ds(18, 14), :] = jnp.zeros((14, 128), F32)
         zsl[half] = zfin[...].astype(BF16)
-        return over_y, z_sends(zsl, rzl, half, S_Z2)
+        return over_y, z_sends(zsl, rzl, half, S_Z2), middle
 
     def last_stage(half, got):
         columns = pl.ds(128 * half, 128)
@@ -455,7 +455,11 @@
     pack(0)
     first0 = first_stage(0)
     arrived(got_ch)
-    pay[:, pl.ds(0, 256)] = add_up(chr_, NC)
+    small = add_up(chr_, NC)
+    rest = small[64:]
+    pay[:, pl.ds(0, 128)] = small[:64]
+    pay[pl.ds(0, 32), pl.ds(128, 128)] = rest
+    pay[pl.ds(32, 32), pl.ds(128, 128)] = jnp.concatenate([rest[:, 64:], rest[:, :64]], axis=1)
     pay[pl.ds(61, 1), pl.ds(0, 128)] = g2acc[:, :128]
     pay[pl.ds(62, 1), pl.ds(0, 128)] = g2acc[:, 128:]
     for k in range(NX):
@@ -474,18 +478,23 @@
     half_grad(1)
     pack(1)
     first1 = first_stage(1)
-    second0 = second_stage(0, first0)
+    second0 = second_stage(0, first0, lambda: None)
     arrived(got_ry)
     rzs[z] = add_up(rys, NY).astype(BF16)
     got_rz = [
         send(rzs.at[z], rzs.at[z], S_RZ + k - 1, (seq_of(y, x, z_peer(k)), c)) for k in range(1, NZ)
     ]
-    second1 = second_stage(1, first1)
-    arrived(got_rz)
-    rgs[x] = add_up(rzs, NZ)
-    got_rg = [
-        send(rgs.at[x], rgs.at[x], S_RG + k - 1, (seq_of(y, x_peer(k), z), c)) for k in range(1, NX)
-    ]
+
+    def gather_small():
+        arrived(got_rz)
+        rgs[x] = add_up(rzs, NZ)
+        return [
+            send(rgs.at[x], rgs.at[x], S_RG + k - 1, (seq_of(y, x_peer(k), z), c))
+            for k in range(1, NX)
+        ]
+
+    second1 = second_stage(1, first1, gather_small)
+    got_rg = second1[2]
     last_stage(0, second0)
     last_stage(1, second1)
     arrived(got_rg)
@@ -563,8 +572,8 @@
             V((ROWS, D1), BF16),
             V((ROWS, D1), BF16),
             V((64, D1), F32),
-            V((NC, 64, 256), BF16),
-            V((NC, 64, 256), BF16),
+            V((NC, 96, 128), BF16),
+            V((NC, 96, 128), BF16),
             V((NX, 16, 256), BF16),
             V((NX, 16, 256), BF16),
             V((NY, 16, 256), BF16),

time: 63.7 us -> 65.1 us (1.022)
  Pallas kernels: 62.9 us -> 64.3 us
    pallas_call x1, Pallas kernels: 61.2 us -> 62.5 us  [on_device(): pl.pallas_call(kernel, out_shape=(jax.ShapeDtypeStruct((ROWS, OWN2), BF16...]
where the time goes in v5:
time: 65.1 us; the launch traced here: 64.9 us
  Pallas kernels  64.3 us (99%)
    pallas_call x1, Pallas kernels, on_device(): pl.pallas_call(kernel, out_shape=(jax.ShapeDtypeStruct((ROWS, OWN2), BF16...  62.5 us
    pallas_call x1, Pallas kernels, on_device(): pl.pallas_call(write_out, out_shape=tuple((jax.ShapeDtypeStruct(r.shape,...  1.75 us

profile of v5, /device:TPU:8, one launch (start us, length us, event | category | flops | bytes accessed | tf_op | source)
XLA Modules:
  0.0 64.9 jit_solution(7010491936869561404)
XLA Ops:
  0.6 62.5 %shard_map.101 = (bf16[384,256]{1,0:T(8,128)(2,1)}, f32[15,4,192]{2,1,0:T(4,128)}, f32[192]{0:T(256)}, f32[5,6,256]{2,1,0:T(8,128)}, f32[256]{0:T(256)}) custom-call(s32[384]{0:T(512)} %bases_hbm.1, bf16[15,4,192]{2,1,0:T(4,128)(2,1)} %bitcast.7, f32[192]{0:T(256)} %g1_hbm.1, bf16[5,768,256]{2,1,0:T(8,128)(2,1)} %bitcast.4, f32[256]{0:T(256)} %g2_hbm.1, ...), custom_call_target="tpu_custom_call" | custom-call | flops 2264924160 | bytes 4194304 | tf_op jit(solution)/shard_map/pallas_call | solution.py:526
  63.2 1.7 %shard_map.102 = (bf16[384,256]{1,0:T(8,128)(2,1)}, f32[15,4,192]{2,1,0:T(4,128)}, f32[192]{0:T(256)}, f32[5,6,256]{2,1,0:T(8,128)}, f32[256]{0:T(256)}) custom-call(bf16[384,256]{1,0:T(8,128)(2,1)} %get-tuple-element.15.refs_0_, f32[15,4,192]{2,1,0:T(4,128)} %get-tuple-element.16.refs_1_, f32[192]{0:T(256)} %get-tuple-element.17.refs_2_, ...), custom_call_target="tpu_custom_call" | custom-call | tf_op jit(solution)/shard_map/pallas_call | solution.py:612

commit v6 on v4

--- a/solution.py
+++ b/solution.py
@@ -346,10 +346,9 @@
     pay[...] = tn_dot(uu[pl.ds(16, ROWS), :], dc1[...])
     pay[pl.ds(60, 1), :] = g1acc[...] / gain1[...]
     for k in range(NC):
-        chs[k, :, pl.ds(0, 128)] = pay[:, OWN1 * k : OWN1 * k + 128].astype(BF16)
-        chs[k, :, pl.ds(128, 128)] = jnp.concatenate(
-            [pay[:, OWN1 * k + 128 : OWN1 * k + 192], jnp.zeros((64, 64), F32)], axis=1
-        ).astype(BF16)
+        chs[k, pl.ds(0, 64), :] = pay[:, OWN1 * k : OWN1 * k + 128].astype(BF16)
+        rest = pay[:, OWN1 * k + 128 : OWN1 * k + 192]
+        chs[k, pl.ds(64, 32), :] = jnp.concatenate([rest[:32], rest[32:]], axis=1).astype(BF16)
     got_ch = [
         send(chs.at[c_peer(k)], chr_.at[c], S_CH + k - 1, (s, c_peer(k))) for k in (2, 1, 3)
     ]
@@ -455,7 +454,11 @@
     pack(0)
     first0 = first_stage(0)
     arrived(got_ch)
-    pay[:, pl.ds(0, 256)] = add_up(chr_, NC)
+    small = add_up(chr_, NC)
+    rest = small[64:]
+    pay[:, pl.ds(0, 128)] = small[:64]
+    pay[pl.ds(0, 32), pl.ds(128, 128)] = rest
+    pay[pl.ds(32, 32), pl.ds(128, 128)] = jnp.concatenate([rest[:, 64:], rest[:, :64]], axis=1)
     pay[pl.ds(61, 1), pl.ds(0, 128)] = g2acc[:, :128]
     pay[pl.ds(62, 1), pl.ds(0, 128)] = g2acc[:, 128:]
     for k in range(NX):
@@ -563,8 +566,8 @@
             V((ROWS, D1), BF16),
             V((ROWS, D1), BF16),
             V((64, D1), F32),
-            V((NC, 64, 256), BF16),
-            V((NC, 64, 256), BF16),
+            V((NC, 96, 128), BF16),
+            V((NC, 96, 128), BF16),
             V((NX, 16, 256), BF16),
             V((NX, 16, 256), BF16),
             V((NY, 16, 256), BF16),

time: 63.7 us -> 63.5 us (level)
  no operation moved by 1% of the time
where the time goes in v6:
time: 63.5 us; the launch traced here: 63.3 us
  Pallas kernels  62.7 us (99%)
  between operations  0.64 us (1%)
    pallas_call x1, Pallas kernels, on_device(): pl.pallas_call(kernel, out_shape=(jax.ShapeDtypeStruct((ROWS, OWN2), BF16...  60.9 us
    pallas_call x1, Pallas kernels, on_device(): pl.pallas_call(write_out, out_shape=tuple((jax.ShapeDtypeStruct(r.shape,...  1.75 us

profile of v6, /device:TPU:8, one launch (start us, length us, event | category | flops | bytes accessed | tf_op | source)
XLA Modules:
  0.0 63.3 jit_solution(7045385628674819690)
XLA Ops:
  0.6 60.9 %shard_map.101 = (bf16[384,256]{1,0:T(8,128)(2,1)}, f32[15,4,192]{2,1,0:T(4,128)}, f32[192]{0:T(256)}, f32[5,6,256]{2,1,0:T(8,128)}, f32[256]{0:T(256)}) custom-call(s32[384]{0:T(512)} %bases_hbm.1, bf16[15,4,192]{2,1,0:T(4,128)(2,1)} %bitcast.7, f32[192]{0:T(256)} %g1_hbm.1, bf16[5,768,256]{2,1,0:T(8,128)(2,1)} %bitcast.4, f32[256]{0:T(256)} %g2_hbm.1, ...), custom_call_target="tpu_custom_call" | custom-call | flops 2264924160 | bytes 4194304 | tf_op jit(solution)/shard_map/pallas_call | solution.py:520
  61.6 1.7 %shard_map.102 = (bf16[384,256]{1,0:T(8,128)(2,1)}, f32[15,4,192]{2,1,0:T(4,128)}, f32[192]{0:T(256)}, f32[5,6,256]{2,1,0:T(8,128)}, f32[256]{0:T(256)}) custom-call(bf16[384,256]{1,0:T(8,128)(2,1)} %get-tuple-element.15.refs_0_, f32[15,4,192]{2,1,0:T(4,128)} %get-tuple-element.16.refs_1_, f32[192]{0:T(256)} %get-tuple-element.17.refs_2_, ...), custom_call_target="tpu_custom_call" | custom-call | tf_op jit(solution)/shard_map/pallas_call | solution.py:606
